TPU v7x, 256 devices: a whole 4x4x8 slice. The times are simulated.
256 devices in a mesh: cam: 32 (over z, y), pt: 8 (over x, core).
Axes of the slice: x: 4, y: 4, z: 8, core: 2. Of those that a mesh axis runs over, the one named last changes fastest.
Arguments:
- jacobian_cam: float32 [4, 18, 131072], P(None, None, ('cam', 'pt')), may hold values from -2 to 2
- jacobian_pt: float32 [4, 6, 131072], P(None, None, ('cam', 'pt'))
- residuals: float32 [4, 2, 131072], P(None, None, ('cam', 'pt')), may hold values from -8 to 8
- point_inverse: float32 [9, 131072], P(None, ('cam', 'pt')), as said below
- obs_camera: int32 [4, 131072], P(None, ('cam', 'pt')), may hold values from 0 to 32767, as said below
- pair_slot: int32 [4, 4, 131072], P(None, None, ('cam', 'pt')), may hold values from 0 to 12, as said below
- observation_used: int32 [4, 131072], P(None, ('cam', 'pt')), may hold values from 0 to 1, as said below
- pattern: int32 [12, 32768], P(None, ('cam', 'pt')), may hold values from 0 to 32767, as said below
Outputs:
- camera_step: float32 [9, 32768], P(None, ('cam', 'pt'))
- cam_residual: float32 [9, 32768], P(None, ('cam', 'pt'))
- point_step: float32 [3, 131072], P(None, ('cam', 'pt'))
Inputs may be any that keep to these rules, and one draw needn't show every extreme that they name: `obs_camera`: the 4 cameras of a point are distinct and lie within 12 places of one another in the order behind pattern. `pair_slot`: entry [a, b, j] is the place k with pattern[k, obs_camera[a, j]] = obs_camera[b, j], and 12 where a equals b. `observation_used`: among the live observations of the points of one device, at most 16 name cameras of one device's share; some pair of devices reaches it. `pattern`: column i lists 12 distinct cameras other than i; camera i is coupled to j exactly when j is coupled to i. `point_inverse`: the inverse of the identity plus the sum over the point's live observations of Jp^T Jp.
All inputs are finite; a program needn't handle non-finite values.
Results may differ from a plain program's by a relative error of at most 0.0003.
Values sent between devices are 32-bit elements; how exact they have to be, the bound alone decides.
No kernel may reach another device: no remote copies, remote signals or barrier semaphores. Data moves between devices by JAX's collectives and lax.ppermute only.
A program may use at most 128 MiB of HBM per device.

v0:
```python
import functools

import jax
import jax.numpy as jnp
from jax import lax
from jax.experimental import pallas as pl
from jax.experimental.pallas import tpu as pltpu
from jax.sharding import PartitionSpec as P

TRACK = 4
NBR = 12
ITERS = 4
OBS_CAP = 16
DAMPING = 1.0
BOTH = ("cam", "pt")

GROUP = 14
PAIRS = 7
ROWS = 2
SLOTS = GROUP * ROWS
CARRIED = 32
PAIR_ROWS = 3
CELL = 96
F32 = jnp.float32
BF16 = jnp.bfloat16
PARAMS = pltpu.CompilerParams(vmem_limit_bytes=28 * 1024 * 1024)


def iota(shape, dim):
    return lax.broadcasted_iota(jnp.int32, shape, dim)


def quotient(values, divisor):
    return jnp.floor((values.astype(F32) + 0.5) * (1.0 / divisor))


def pieces(values):
    high = values.astype(BF16)
    rest = values - high.astype(F32)
    middle = rest.astype(BF16)
    low = (rest - middle.astype(F32)).astype(BF16)
    return high, middle, low


def dot_nn(left, right):
    return lax.dot_general(left, right, (((1,), (0,)), ((), ())), preferred_element_type=F32)


def dot_nt(left, right):
    return lax.dot_general(left, right, (((1,), (1,)), ((), ())), preferred_element_type=F32)


def one_hot(condition):
    return jnp.where(condition, 1.0, 0.0).astype(BF16)


def before(size):
    return one_hot(iota((size, size), 0) < iota((size, size), 1))


def flat(array):
    tracks, rows, npts = array.shape
    tiles = jnp.transpose(array, (1, 0, 2)).reshape(rows, tracks, npts // 128, 128)
    return jnp.transpose(tiles, (0, 2, 1, 3)).reshape(-1, 128)


def lines(ref, a, first, count, npts):
    tiles = npts // 128
    step = TRACK * tiles
    return jnp.concatenate(
        [ref[pl.ds(step * first + TRACK * t + a, count, stride=step), :] for t in range(tiles)], axis=1
    )


def pack_kernel(
    devices, shift, jc_ref, jp_ref, rs_ref, vi_ref, cam_ref, slot_ref, used_ref, pattern_ref,
    out_ref, place_ref, rank_ref, feat_ref,
):
    npts = cam_ref.shape[1]
    cam_dev = pattern_ref.shape[1]
    found = jnp.zeros((devices, cam_dev), F32)
    for k in range(NBR):
        target = lax.shift_right_logical(pattern_ref[k : k + 1, :], shift)
        found = jnp.where(iota((devices, cam_dev), 0) == target, 1.0, found)
    rank = dot_nn(found.astype(BF16), before(cam_dev))
    rank_ref[...] = jnp.where(found > 0, rank, -1.0e6)
    live = [used_ref[a : a + 1, :].astype(F32) for a in range(TRACK)]
    carry = jnp.zeros((devices, 1), F32)
    triangle = before(npts)
    hits = []
    withins = []
    for a in range(TRACK):
        owner = lax.shift_right_logical(cam_ref[a : a + 1, :], shift)
        hit = jnp.where(
            jnp.logical_and(iota((devices, npts), 0) == owner, live[a] > 0), 1.0, 0.0
        )
        hits.append(hit.astype(BF16))
        count = dot_nn(hits[a], triangle) + carry
        within = jnp.sum(hit * count, axis=0, keepdims=True)
        carry = carry + jnp.sum(hit, axis=1, keepdims=True)
        withins.append(within)
        place_ref[a : a + 1, :] = jnp.where(live[a] > 0, owner.astype(F32), -1.0)
        place_ref[TRACK + a : TRACK + a + 1, :] = within

    vi = [[vi_ref[3 * x + y : 3 * x + y + 1, :] for y in range(3)] for x in range(3)]
    jp = [
        [[gradient[3 * u + x : 3 * u + x + 1] for x in range(3)] for u in range(2)]
        for gradient in [lines(jp_ref, a, 0, 6, npts) for a in range(TRACK)]
    ]
    jc = [lines(jc_ref, a, 0, 18, npts) for a in range(TRACK)]
    res = [[rs_ref[a, u : u + 1, :] for u in range(2)] for a in range(TRACK)]
    grad = []
    for x in range(3):
        total = jnp.zeros((1, npts), F32)
        for a in range(TRACK):
            total = total - live[a] * (jp[a][0][x] * res[a][0] + jp[a][1][x] * res[a][1])
        grad.append(total)
    for a in range(TRACK):
        at = slice(a * npts, (a + 1) * npts)
        for u in range(2):
            feat_ref[8 * u : 8 * u + 8, at] = jc[a][9 * u : 9 * u + 8]
            feat_ref[64 + u : 65 + u, at] = jc[a][9 * u + 8 : 9 * u + 9]
        removed = [
            [live[a] * sum(jp[a][u][x] * vi[x][y] for x in range(3)) for y in range(3)]
            for u in range(2)
        ]

        def middle(b, u, v):
            return -live[b] * sum(removed[u][y] * jp[b][v][y] for y in range(3))

        partners = [b for b in range(TRACK) if b != a]
        for m, b in enumerate(partners):
            first = [jc[b][9 * v : 9 * v + 8] for v in range(2)]
            ninth = [jc[b][9 * v + 8 : 9 * v + 9] for v in range(2)]
            for u in range(2):
                row = 2 + 2 * m + u
                one, two = middle(b, u, 0), middle(b, u, 1)
                feat_ref[8 * row : 8 * row + 8, at] = one * first[0] + two * first[1]
                feat_ref[64 + row : 65 + row, at] = one * ninth[0] + two * ninth[1]
        feat_ref[72:73, at] = live[a] + middle(a, 0, 0)
        feat_ref[73:74, at] = middle(a, 0, 1)
        feat_ref[74:75, at] = live[a] + middle(a, 1, 1)
        for u in range(2):
            right = -(live[a] * res[a][u] + sum(removed[u][y] * grad[y] for y in range(3)))
            feat_ref[75 + u : 76 + u, at] = right
        own = cam_ref[a : a + 1, :] & (cam_dev - 1)
        for m, b in enumerate(partners):
            label = slot_ref[a, b : b + 1, :] * cam_dev + own
            feat_ref[77 + m : 78 + m, at] = label.astype(F32)

    owners = jnp.concatenate(hits, axis=1)
    place = jnp.concatenate(withins, axis=1)
    split = pieces(feat_ref[...])
    masks = [
        one_hot(jnp.broadcast_to(place, (16, TRACK * npts)) == float(s)) for s in range(OBS_CAP)
    ]
    for g in range(5):
        right = jnp.concatenate(
            [
                part[16 * g : 16 * g + 16] * masks[8 * h + c]
                for h in range(2) for part in split for c in range(8)
            ],
            axis=0,
        )
        sums = dot_nt(owners, right)
        for h in range(2):
            mine = sums[:, 384 * h : 384 * h + 384]
            out_ref[pl.ds(2 * g + h, devices, stride=10), :] = (
                mine[:, :128] + mine[:, 128:256] + mine[:, 256:]
            )


def place_kernel(devices, shift, pattern_ref, rank_ref, source_ref, far_ref, back_ref, choice_ref, count_ref):
    cam_dev = pattern_ref.shape[1]
    turned = rank_ref[...].T
    camera = iota(turned.shape, 0).astype(F32)
    for h in range(ROWS):
        for g in range(16):
            here = jnp.where(turned == float(GROUP * h + g), camera, 0.0)
            choice_ref[16 * h + g : 16 * h + g + 1, :] = jnp.sum(here, axis=0, keepdims=True).astype(jnp.int32)
    most = jnp.sum(jnp.where(turned >= 0, 1.0, 0.0), axis=0, keepdims=True)
    carried = total_of(jnp.maximum(2.0 * most - SLOTS, 0.0))
    full = jnp.max(most, axis=1, keepdims=True)
    crowded = jnp.where(jnp.logical_or(full > float(SLOTS), carried > float(CARRIED)), 1.0, 0.0)
    count_ref[0:1, :] = most
    count_ref[1:2, :] = jnp.zeros_like(most) + crowded
    count = jnp.zeros((devices, cam_dev), F32)
    sources = []
    withins = []
    for k in range(NBR):
        camera = pattern_ref[k : k + 1, :]
        source = lax.shift_right_logical(camera, shift)
        within = camera & (cam_dev - 1)
        sources.append(iota((devices, cam_dev), 0) == source)
        withins.append(iota((cam_dev, cam_dev), 0) == within)
        count = count + dot_nt(one_hot(sources[k]), one_hot(withins[k]))
        source_ref[:, k * cam_dev : (k + 1) * cam_dev] = source.astype(F32)
    found = one_hot(count > 0)
    rank = dot_nn(found, before(cam_dev))
    most = jnp.sum(found.astype(F32), axis=1, keepdims=True)
    turned = rank.T.astype(BF16)
    for k in range(NBR):
        column = dot_nn(turned, one_hot(sources[k]))
        mine = jnp.sum(jnp.where(withins[k], column, 0.0), axis=0, keepdims=True)
        far_ref[:, k * cam_dev : (k + 1) * cam_dev] = mine
        full = jnp.sum(jnp.where(sources[k], most, 0.0), axis=0, keepdims=True)
        back = SLOTS - 1.0 - mine
        back_ref[:, k * cam_dev : (k + 1) * cam_dev] = jnp.where(back >= full, back, -1.0)


def outer(left, right):
    blocks = []
    for r in range(8):
        blocks.append(left[0][0][r : r + 1] * right[0][0] + left[1][0][r : r + 1] * right[1][0])
    blocks.append(left[0][1] * right[0][0] + left[1][1] * right[1][0])
    blocks.append(left[0][0] * right[0][1] + left[1][0] * right[1][1])
    return blocks, left[0][1] * right[0][1] + left[1][1] * right[1][1]


def turn(got_ref, text_ref, parts):
    devices = got_ref.shape[0] // 10
    for h in range(2):
        for row, g in enumerate(parts):
            turned = got_ref[pl.ds(2 * g + h, devices, stride=10), :].T
            for c in range(8):
                at = slice((c % 2) * devices, (c % 2 + 1) * devices)
                text_ref[4 * h + c // 2, 16 * row : 16 * row + 16, at] = turned[16 * c : 16 * c + 16]


def observation(text, cam_dev):
    own = [(text[8 * u : 8 * u + 8], text[16 + u : 17 + u]) for u in range(2)]
    cells = [quotient(text[29 + m : 30 + m], cam_dev) for m in range(3)]
    within = text[29:30] - cells[0] * cam_dev
    hit = one_hot(iota((cam_dev, text.shape[1]), 0).astype(F32) == within)
    return own, cells, hit


def folded(sums):
    size = sums.shape[0] // 3
    return sums[:size] + sums[size : 2 * size] + sums[2 * size :]


def diagonal_kernel(
    got_ref, choice_ref, count_ref, text_ref, out_ref, lower_ref, state_ref, send_ref
):
    cam_dev = out_ref.shape[1]
    turn(got_ref, text_ref, (0, 4))
    unit = iota((CELL, cam_dev), 0)
    unit = jnp.logical_and(unit <= 63, unit == 9 * lax.shift_right_logical(unit, 3)) | (unit == 80)
    total = jnp.where(unit, DAMPING, 0.0)
    for index in range(OBS_CAP // 2):
        text = text_ref[index]
        own, _, hit = observation(text, cam_dev)
        corner = [[text[24:25], text[25:26]], [text[25:26], text[26:27]]]
        weighted = [
            tuple(corner[u][0] * own[0][i] + corner[u][1] * own[1][i] for i in range(2)) for u in range(2)
        ]
        blocks, edge = outer(own, weighted)
        extra = [text[27:28], text[28:29]]
        ninth = own[0][1] * extra[0] + own[1][1] * extra[1]
        blocks.append(jnp.concatenate([edge, ninth, jnp.zeros((6, text.shape[1]), F32)], axis=0))
        blocks.append(own[0][0] * extra[0] + own[1][0] * extra[1])
        term = jnp.concatenate(blocks, axis=0)
        total = total + folded(dot_nt(jnp.concatenate(pieces(term), axis=0), hit))
    out_ref[...] = total
    cholesky(out_ref, lower_ref)
    right = jnp.concatenate([total[88:96], total[81:82], jnp.zeros((7, cam_dev), F32)], axis=0)
    scaled = solve(lower_ref, right)
    zero = jnp.zeros_like(right)
    state_ref[0] = zero
    state_ref[1] = right
    state_ref[2] = scaled
    state_ref[3] = scaled
    for index in range(4, 7):
        state_ref[index] = zero
    send_rows(send_ref, coupled(scaled, None, choice_ref, count_ref), [count_ref[1:2, :1]])


def coupling_kernel(got_ref, text_ref, lower_ref, out_ref, wanted_ref, inverse_ref, edge_ref, more_ref):
    cam_dev = out_ref.shape[2]
    devices = wanted_ref.shape[1]
    out_ref[...] = jnp.zeros_like(out_ref)
    edge_ref[...] = jnp.zeros_like(edge_ref)
    turn(got_ref, more_ref, (1, 2, 3))

    def step(index, _):
        text, more = text_ref[index], more_ref[index]
        own, cells, hit = observation(text, cam_dev)
        partners = [(more[8 * v : 8 * v + 8], text[18 + v : 19 + v]) for v in range(6)]
        terms, edges = [], jnp.zeros((16, hit.shape[1]), F32)
        row = iota(edges.shape, 0).astype(F32)
        for m in range(3):
            blocks, edge = outer(own, partners[2 * m : 2 * m + 2])
            terms.append(jnp.concatenate(pieces(jnp.concatenate(blocks, axis=0)), axis=0))
            edges = jnp.where(row == cells[m], edge, edges)
        for k in range(NBR):
            part = None
            for m in range(3):
                piece = terms[m] * one_hot(cells[m] == float(k))
                part = piece if part is None else part + piece
            out_ref[k, :80] = out_ref[k, :80] + folded(dot_nt(part, hit))
        edge_ref[...] = edge_ref[...] + folded(dot_nt(jnp.concatenate(pieces(edges), axis=0), hit))
        return 0

    lax.fori_loop(0, OBS_CAP // 2, step, 0, unroll=True)
    for k in range(NBR):
        out_ref[k, 80:81] = edge_ref[k : k + 1]
    for s in range(OBS_CAP):
        label = text_ref[s // 2, 29:30, (s % 2) * devices : (s % 2 + 1) * devices]
        wanted_ref[s : s + 1, :] = (label - cam_dev * quotient(label, cam_dev)).astype(jnp.int32)
    row = iota((16, 9 * cam_dev), 0)
    unit = lax.shift_right_logical(iota((16, 9 * cam_dev), 1), cam_dev.bit_length() - 1) == row
    solved = solve(lower_ref, jnp.where(unit, 1.0, 0.0))
    columns = [solved[:, c * cam_dev : (c + 1) * cam_dev] for c in range(9)]
    inverse_ref[...] = jnp.concatenate(
        [column[:8] for column in columns] + [columns[8][:8], columns[8][8:], jnp.zeros((8, cam_dev), F32)],
        axis=0,
    )


def cholesky(cells_ref, lower_ref):
    cam_dev = cells_ref.shape[1]
    zero = jnp.zeros((7, cam_dev), F32)
    block = cells_ref[...]
    columns = [
        jnp.concatenate([block[8 * r : 8 * r + 8], block[64 + r : 65 + r], zero], axis=0) for r in range(8)
    ]
    columns.append(jnp.concatenate([block[64:72], block[80:81], zero], axis=0))
    row = iota((16, cam_dev), 0)
    for c in range(9):
        pivot = columns[c][c : c + 1]
        root = jnp.sqrt(pivot)
        inverse = 1.0 / root
        column = jnp.where(row > c, columns[c] * inverse, 0.0)
        for r in range(c + 1, 9):
            columns[r] = columns[r] - column * column[r : r + 1]
        lower_ref[c] = jnp.where(row == 9, inverse, jnp.where(row < 9, column, 0.0))


def solve(lower_ref, vector):
    row = iota(vector.shape, 0)
    rest = vector
    copies = vector.shape[1] // lower_ref.shape[2]
    columns = [jnp.concatenate([lower_ref[c]] * copies, axis=1) for c in range(9)]
    for c in range(9):
        column = columns[c]
        value = rest[c : c + 1] * column[9:10]
        rest = jnp.where(row == c, value, rest - jnp.where(row < 9, column, 0.0) * value)
    for c in reversed(range(9)):
        column = columns[c]
        if c < 8:
            dotted = jnp.sum(
                jnp.where(jnp.logical_and(row > c, row < 9), column * rest, 0.0), axis=0, keepdims=True
            )
        else:
            dotted = jnp.zeros((1, vector.shape[1]), F32)
        value = (rest[c : c + 1] - dotted) * column[9:10]
        rest = jnp.where(row == c, value, rest)
    return rest


def multiply(pairs):
    cam_dev = pairs[0][1].shape[1]
    sums = [jnp.zeros((8, cam_dev), F32) for _ in range(9)]
    side = jnp.zeros((8, cam_dev), F32)
    corner = jnp.zeros((1, cam_dev), F32)
    for cell_ref, vector in pairs:
        first, last = vector[0:8], vector[8:9]
        for r in range(9):
            sums[r] = sums[r] + cell_ref[8 * r : 8 * r + 8, :] * first
        side = side + cell_ref[72:80, :] * last
        corner = corner + cell_ref[80:81, :] * last
    sums = [jnp.sum(part, axis=0, keepdims=True) for part in sums]
    top = jnp.concatenate(sums[:8], axis=0) + side
    return jnp.concatenate([top, sums[8] + corner, jnp.zeros((7, cam_dev), F32)], axis=0)


def total_of(values):
    return jnp.sum(jnp.sum(values, axis=1, keepdims=True), axis=0, keepdims=True)


FIRST = 8


def chosen(values, cameras):
    width = values.shape[1]
    return jnp.concatenate(
        [
            jnp.take_along_axis(values, cameras[:, at : at + width], axis=1, mode="promise_in_bounds")
            for at in range(0, cameras.shape[1], width)
        ],
        axis=1,
    )


def spread(row):
    return jnp.broadcast_to(row, (8, row.shape[1]))


def message(firsts, ninths):
    return jnp.concatenate(firsts[:FIRST] + ninths[:1] + firsts[FIRST:] + ninths[1:], axis=0)


def camera_rows(vector, choice_ref, order):
    cameras = [choice_ref[at : at + 1, :] for at in order]
    firsts = [chosen(vector[:8], spread(row)) for row in cameras]
    last = spread(vector[8:9])
    blank = jnp.zeros_like(cameras[0])
    ninths = [
        chosen(last, jnp.concatenate(cameras[:FIRST], axis=0)),
        chosen(last, jnp.concatenate(cameras[FIRST:] + [blank, blank], axis=0)),
    ]
    return message(firsts, ninths)


def coupled(vector, second, choice_ref, count_ref):
    texts = [camera_rows(vector, choice_ref, range(16 * h, 16 * h + GROUP)) for h in range(ROWS)]
    if second is not None:
        others = camera_rows(second, choice_ref, range(GROUP - 1, -1, -1))
        lane = iota(others.shape, 0)
        low = jnp.where(lane < 64, lax.shift_right_logical(lane, 3), lane - 64)
        high = FIRST + jnp.where(lane < 120, lax.shift_right_logical(lane - 72, 3), lane - 120)
        place = GROUP * (ROWS - 1) + jnp.where(lane < 72, low, high)
        texts[-1] = jnp.where(place.astype(F32) >= count_ref[0:1, :], others, texts[-1])
    return texts


def observed(one, two, wanted_ref):
    even = iota((8, one.shape[1]), 0) & 1
    last = jnp.where(even == 0, spread(one[8:9]), spread(two[8:9]))
    blank = jnp.zeros((1, wanted_ref.shape[1]), jnp.int32)
    texts = []
    for h in range(PAIR_ROWS):
        slots = [PAIRS * h + g for g in range(PAIRS)]
        cameras = [wanted_ref[slot : slot + 1, :] if slot < OBS_CAP else blank for slot in slots]
        firsts = [chosen(vector[:8], spread(row)) for row in cameras for vector in (one, two)]
        double = [row for row in cameras for _ in range(2)] + [blank, blank]
        ninths = [chosen(last, jnp.concatenate(double[at : at + 8], axis=0)) for at in (0, 8)]
        texts.append(message(firsts, ninths))
    return texts


def send_rows(send_ref, texts, scalars):
    rows = len(texts)
    devices = send_ref.shape[0] // rows
    for h, text in enumerate(texts):
        lane = iota(text.shape, 0)
        for index, scalar in enumerate(scalars[2 * h : 2 * h + 2]):
            text = jnp.where(lane == 126 + index, scalar, text)
        send_ref[pl.ds(h, devices, stride=rows), :] = text.T


def read_rows(got_ref, rows, sources):
    devices = got_ref.shape[0] // rows
    turned = [got_ref[pl.ds(h, devices, stride=rows), :].T for h in range(rows)]
    mark = one_hot(iota((devices, sources.shape[1]), 0).astype(F32) == sources)
    split = jnp.concatenate([piece for plane in turned for piece in pieces(plane)], axis=0)
    taken = dot_nn(split, mark)
    taken = [
        taken[at : at + 128] + taken[at + 128 : at + 256] + taken[at + 256 : at + 384]
        for at in range(0, 384 * rows, 384)
    ]
    sums = [jnp.sum(plane[126 + i : 127 + i], axis=1, keepdims=True) for plane in turned for i in range(2)]
    return taken, sums


def pick(taken, groups):
    top = jnp.zeros((8, taken.shape[1]), F32)
    for g in range(GROUP):
        at = 8 * g if g < FIRST else 8 * g + 8
        top = jnp.where(groups == float(g), taken[at : at + 8], top)
    row = iota((8, taken.shape[1]), 0).astype(F32)
    ninth = jnp.where(row == groups, taken[64:72], jnp.where(row + FIRST == groups, taken[120:128], 0.0))
    ninth = jnp.sum(ninth, axis=0, keepdims=True)
    return jnp.concatenate([top, ninth, jnp.zeros((7, taken.shape[1]), F32)], axis=0)


def step_kernel(
    index, got_ref, source_ref, place_ref, second_ref, choice_ref, count_ref, cells_ref, diagonal_ref, inverse_ref,
    state_ref, far_ref, state_out, far_out, send_ref,
):
    (upper, lower), sums = read_rows(got_ref, ROWS, source_ref[...])
    place = place_ref[...]
    part = quotient(place, GROUP)
    arrived = pick(jnp.where(part == 0, upper, lower), place - part * GROUP)
    step, rest, scaled, direction = (state_ref[i] for i in range(4))
    if index:
        image, image_scaled = state_ref[4], state_ref[5]
        energy, cross, square, old = sums
        alpha = old / energy
        beta = (old - 2.0 * alpha * cross + alpha * alpha * square) / old
        step = step + alpha * direction
        rest = rest - alpha * image
        direction = (scaled - alpha * image_scaled) + beta * direction
        far_before = far_ref[1]
        if index >= 2:
            second = second_ref[...]
            far_before = jnp.where(second >= 0, pick(lower, second - GROUP), far_before)
        far_scaled = far_before - alpha * arrived
        far = far_scaled + beta * far_ref[0]
    else:
        far_scaled = arrived
        far = arrived
    cam_dev = cells_ref.shape[2]
    image = multiply(
        [(diagonal_ref, direction)]
        + [(cells_ref.at[k], far[:, k * cam_dev : (k + 1) * cam_dev]) for k in range(NBR)]
    )
    energy = total_of(direction * image)
    scaled = multiply([(inverse_ref, rest)]) if index else scaled
    old = total_of(rest * scaled)
    state_out[0] = step
    state_out[1] = rest
    state_out[2] = scaled
    state_out[3] = direction
    state_out[4] = image
    state_out[6] = state_ref[6] if index else jnp.zeros_like(step) + sums[0]
    far_out[0] = far
    far_out[1] = far_scaled
    if index == ITERS - 1:
        state_out[5] = jnp.zeros_like(image)
        send_rows(send_ref, observed(step, direction, choice_ref), [energy, old])
        return
    image_scaled = multiply([(inverse_ref, image)])
    state_out[5] = image_scaled
    scalars = [energy, total_of(scaled * image), total_of(image * image_scaled), old]
    second = scaled if index + 1 >= 2 else None
    send_rows(send_ref, coupled(image_scaled, second, choice_ref, count_ref), scalars)


def finish_kernel(
    got_ref, place_ref, state_ref, jc_ref, jp_ref, rs_ref, vi_ref, used_ref, step_ref, rest_ref, point_ref
):
    npts = used_ref.shape[1]
    places = jnp.concatenate([place_ref[a : a + 1, :] for a in range(TRACK)], axis=1)
    within = jnp.concatenate([place_ref[TRACK + a : TRACK + a + 1, :] for a in range(TRACK)], axis=1)
    taken, sums = read_rows(got_ref, PAIR_ROWS, places)
    energy, old = sums[:2]
    alpha = old / energy
    step_ref[...] = (state_ref[0] + alpha * state_ref[3])[:9]
    rest_ref[...] = (state_ref[1] - alpha * state_ref[4])[:9]
    part = quotient(within, PAIRS)
    taken = jnp.where(part == 0, taken[0], jnp.where(part == 1, taken[1], taken[2]))
    groups = 2.0 * (within - part * PAIRS)
    moved = pick(taken, groups) + alpha * pick(taken, groups + 1.0)
    reduced = [jnp.zeros((1, npts), F32) for _ in range(3)]
    for a in range(TRACK):
        live = used_ref[a : a + 1, :].astype(F32)
        there = moved[:9, a * npts : (a + 1) * npts]
        jacobian = lines(jc_ref, a, 0, 18, npts)
        gradient = lines(jp_ref, a, 0, 6, npts)
        for u in range(2):
            change = jnp.sum(jacobian[9 * u : 9 * u + 9] * there, axis=0, keepdims=True)
            change = live * (change + rs_ref[a, u : u + 1, :])
            for x in range(3):
                reduced[x] = reduced[x] - gradient[3 * u + x : 3 * u + x + 1] * change
    for x in range(3):
        point_ref[x : x + 1, :] = sum(
            vi_ref[3 * x + y : 3 * x + y + 1, :] * reduced[y] for y in range(3)
        )


def factor_blocks(matrix):
    lower = {}
    for row_idx in range(9):
        for col_idx in range(row_idx + 1):
            accum = matrix[row_idx, col_idx]
            for inner_idx in range(col_idx):
                accum = accum - lower[row_idx, inner_idx] * lower[col_idx, inner_idx]
            if row_idx == col_idx:
                lower[row_idx, row_idx] = jnp.sqrt(accum)
            else:
                lower[row_idx, col_idx] = accum / lower[col_idx, col_idx]
    return lower


def solve_blocks(lower, vector):
    forward = []
    for row_idx in range(9):
        accum = vector[row_idx]
        for inner_idx in range(row_idx):
            accum = accum - lower[row_idx, inner_idx] * forward[inner_idx]
        forward.append(accum / lower[row_idx, row_idx])
    backward = [None] * 9
    for row_idx in reversed(range(9)):
        accum = forward[row_idx]
        for inner_idx in range(row_idx + 1, 9):
            accum = accum - lower[inner_idx, row_idx] * backward[inner_idx]
        backward[row_idx] = accum / lower[row_idx, row_idx]
    return jnp.stack(backward)


def whole_exchange(cells, diagonal, pattern, jacobian_cam, jacobian_pt, residuals, point_inverse, obs_camera, used):
    cam_dev = pattern.shape[1]
    cells = jnp.concatenate([cells, diagonal[None]], axis=0)
    main = cells[:, :64].reshape(NBR + 1, 8, 8, cam_dev)
    side = cells[:, 72:80].reshape(NBR + 1, 8, 1, cam_dev)
    foot = jnp.concatenate([cells[:, 64:72], cells[:, 80:81]], axis=1)[:, None]
    blocks = jnp.concatenate([jnp.concatenate([main, side], axis=2), foot], axis=1)
    gradient = jnp.concatenate([cells[NBR, 88:96], cells[NBR, 81:82]], axis=0)
    lower = factor_blocks(blocks[NBR])

    def gathered(vector):
        return lax.all_gather(vector, BOTH, axis=1, tiled=True)

    def summed(values):
        return lax.psum(jnp.sum(values), BOTH)

    step = jnp.zeros_like(gradient)
    rest = gradient
    scaled = solve_blocks(lower, rest)
    direction = scaled
    energy_now = summed(rest * scaled)
    for _ in range(ITERS):
        taken = jnp.concatenate([gathered(direction)[:, pattern], direction[:, None, :]], axis=1)
        image = jnp.sum(blocks * jnp.swapaxes(taken, 0, 1)[:, None], axis=(0, 2))
        alpha = energy_now / summed(direction * image)
        step = step + alpha * direction
        rest = rest - alpha * image
        scaled = solve_blocks(lower, rest)
        energy_next = summed(rest * scaled)
        direction = scaled + energy_next / energy_now * direction
        energy_now = energy_next
    whole = gathered(step)
    npts = obs_camera.shape[1]
    rows = jacobian_cam.reshape(TRACK, 2, 9, npts)
    seen = jnp.swapaxes(whole[:, obs_camera], 0, 1)
    change = jnp.sum(rows * seen[:, None], axis=2) + residuals
    change = change * used.astype(F32)[:, None]
    reduced = -jnp.sum(jacobian_pt.reshape(TRACK, 2, 3, npts) * change[:, :, None], axis=(0, 1))
    point_step = jnp.sum(point_inverse.reshape(3, 3, npts) * reduced[None], axis=1)
    return step, rest, point_step


def shape(*dims, dtype=F32):
    return jax.ShapeDtypeStruct(dims, dtype)


def call(kernel, outs, name, scratch=(), flops=0):
    cost = pl.CostEstimate(flops=flops, bytes_accessed=1 << 20, transcendentals=0) if flops else None
    return pl.pallas_call(
        kernel, out_shape=outs, name=name, compiler_params=PARAMS, scratch_shapes=list(scratch),
        cost_estimate=cost,
    )


def exchange(message, devices):
    width = message.shape[0] // devices
    arrived = lax.all_to_all(
        message.reshape(devices, width, 1, 128), BOTH, split_axis=0, concat_axis=0, tiled=True
    )
    return arrived.reshape(devices * width, 128)


def per_device(
    jacobian_cam, jacobian_pt, residuals, point_inverse, obs_camera, pair_slot, observation_used, pattern,
):
    devices = lax.axis_size("cam") * lax.axis_size("pt")
    npts = obs_camera.shape[1]
    cam_dev = pattern.shape[1]
    shift = cam_dev.bit_length() - 1
    couplings = NBR * cam_dev

    cameras = flat(jacobian_cam)
    points = flat(jacobian_pt)

    packed, places, rank = call(
        functools.partial(pack_kernel, devices, shift),
        (
            shape(devices * 10, 128), shape(2 * TRACK, npts), shape(devices, cam_dev),
        ),
        "pack",
        [pltpu.VMEM((80, TRACK * npts), F32)],
    )(cameras, points, residuals, point_inverse, obs_camera, pair_slot, observation_used, pattern)
    got = exchange(packed, devices)
    sources, far_rank, far_back, choice, count = call(
        functools.partial(place_kernel, devices, shift),
        (
            shape(1, couplings),
            shape(1, couplings),
            shape(1, couplings),
            shape(16 * ROWS, devices, dtype=jnp.int32),
            shape(2, devices),
        ),
        "place",
        flops=4 * 10**9,
    )(pattern, rank)
    text, diagonal, lower, state, message = call(
        diagonal_kernel,
        (
            shape(OBS_CAP // 2, 32, 2 * devices),
            shape(CELL, cam_dev),
            shape(9, 16, cam_dev),
            shape(7, 16, cam_dev),
            shape(devices * ROWS, 128),
        ),
        "diagonal",
    )(got, choice, count)
    cells, wanted, inverse = call(
        coupling_kernel,
        (shape(NBR, CELL, cam_dev), shape(OBS_CAP, devices, dtype=jnp.int32), shape(CELL, cam_dev)),
        "coupling",
        [pltpu.VMEM((16, cam_dev), F32), pltpu.VMEM((OBS_CAP // 2, 48, 2 * devices), F32)],
        flops=8 * 10**9,
    )(got, text, lower)
    far = jnp.zeros((2, 16, couplings), F32)
    crowded = None
    for index in range(ITERS):
        last = index == ITERS - 1
        rows = PAIR_ROWS if last else ROWS
        arrived = exchange(message, devices)
        state, far, message = call(
            functools.partial(step_kernel, index),
            (shape(7, 16, cam_dev), shape(2, 16, couplings), shape(devices * rows, 128)),
            "step",
        )(
            arrived, sources, far_rank, far_back, wanted if last else choice, count, cells, diagonal, inverse,
            state, far,
        )
        if index == 0:
            crowded = state[6, 0, 0] > 0.0
    arrived = exchange(message, devices)
    found = call(
        finish_kernel, (shape(9, cam_dev), shape(9, cam_dev), shape(3, npts)), "finish"
    )(arrived, places, state, cameras, points, residuals, point_inverse, observation_used)

    def dense():
        return whole_exchange(
            cells, diagonal, pattern, jacobian_cam, jacobian_pt, residuals, point_inverse, obs_camera, observation_used
        )

    return lax.cond(crowded, dense, lambda: tuple(found))


def solution(mesh):
    return jax.shard_map(
        per_device,
        mesh=mesh,
        in_specs=(
            P(None, None, BOTH),
            P(None, None, BOTH),
            P(None, None, BOTH),
            P(None, BOTH),
            P(None, BOTH),
            P(None, None, BOTH),
            P(None, BOTH),
            P(None, BOTH),
        ),
        out_specs=(P(None, BOTH), P(None, BOTH), P(None, BOTH)),
        check_vma=False,
    )
```

profile of v0, /device:TPU:1, one launch (start us, length us, event | category | flops | bytes accessed | tf_op | source)
XLA Modules:
  0.0 207.2 jit_solution(3365792115342538477)
XLA Ops:
  7.2 0.0 copy-start
  7.2 0.7 copy-done
  7.9 7.4 %pack.1 = (f32[2560,128]{1,0:T(8,128)}, f32[8,512]{1,0:T(8,128)S(1)}, f32[256,128]{1,0:T(8,128)S(1)}) custom-call(f32[288,128]{1,0:T(8,128)} %bitcast.633, f32[96,128]{1,0:T(8,128)} %bitcast.641, f32[4,2,512]{2,1,0:T(2,128)} %rs_ref.3, f32[9,512]{1,0:T(8,128)} %vi_ref.3, s32[4,512]{1,0:T(4,128)} %cam_ref.1, s32[4,4,512]{2,1,0:T(4,128)S(1)} %copy-done, ...), custom_call_target="tpu_custom_call" | custom-call | tf_op jit(solution)/shard_map/pack/pallas_call | solution.py:667
  15.3 15.7 %all-to-all-start = ((f32[256,10,1,128]{3,2,1,0:T(1,128)}), f32[256,10,1,128]{3,2,1,0:T(1,128)S(1)}, u32[]{:S(2)}, u32[]{:S(2)}) async-start(f32[256,10,1,128]{3,2,1,0:T(1,128)} %bitcast.117), calls=%async_computation | async-start | bytes 2621440 | tf_op jit(solution)/shard_map/all_to_all | solution.py:649
  31.0 2.1 %place.1 = (f32[1,1536]{1,0:T(1,128)S(1)}, f32[1,1536]{1,0:T(1,128)S(1)}, f32[1,1536]{1,0:T(1,128)S(1)}, s32[32,256]{1,0:T(8,128)S(1)}, f32[2,256]{1,0:T(2,128)S(1)}) custom-call(s32[12,128]{1,0:T(8,128)} %pattern_ref.3, f32[256,128]{1,0:T(8,128)S(1)} %get-tuple-element.64.rank_ref), custom_call_target="tpu_custom_call" | custom-call | flops 4000000000 | bytes 1048576 | tf_op jit(solution)/shard_map/place/pallas_call | solution.py:676
  33.1 33.9 %all-to-all-done = f32[256,10,1,128]{3,2,1,0:T(1,128)S(1)} async-done(((f32[256,10,1,128]{3,2,1,0:T(1,128)}), f32[256,10,1,128]{3,2,1,0:T(1,128)S(1)}, u32[]{:S(2)}, u32[]{:S(2)}) %all-to-all-start) | async-done | bytes 1310752 | tf_op jit(solution)/shard_map/all_to_all | solution.py:649
  67.0 2.3 %diagonal.1 = (f32[8,32,512]{2,1,0:T(8,128)S(1)}, f32[96,128]{1,0:T(8,128)S(1)}, f32[9,16,128]{2,1,0:T(8,128)S(1)}, f32[7,16,128]{2,1,0:T(8,128)S(1)}, f32[512,128]{1,0:T(8,128)}) custom-call(f32[2560,128]{1,0:T(8,128)S(1)} %bitcast.609, s32[32,256]{1,0:T(8,128)S(1)} %get-tuple-element.65.choice_ref, f32[2,256]{1,0:T(2,128)S(1)} %get-tuple-element.66.count_ref), custom_call_target="tpu_custom_call" | custom-call | tf_op jit(solution)/shard_map/diagonal/pallas_call | solution.py:688
  69.3 7.0 %all-to-all-start.1 = ((f32[256,2,1,128]{3,1,2,0:T(2,128)}), f32[256,2,1,128]{3,1,2,0:T(2,128)S(1)}, u32[]{:S(2)}, u32[]{:S(2)}) async-start(f32[256,2,1,128]{3,1,2,0:T(2,128)} %bitcast.120), calls=%async_computation.1 | async-start | bytes 524288 | tf_op jit(solution)/shard_map/all_to_all | solution.py:649
  76.3 0.0 copy-start.1
  76.3 0.0 copy-start.2
  76.3 0.0 copy-start.3
  76.3 0.0 copy-start.7
  76.3 0.0 copy-start.9
  76.3 0.0 copy-start.10
  76.4 0.0 copy-start.11
  76.4 7.8 %coupling.1 = (f32[12,96,128]{2,1,0:T(8,128)S(1)}, s32[16,256]{1,0:T(8,128)S(1)}, f32[96,128]{1,0:T(8,128)S(1)}) custom-call(f32[2560,128]{1,0:T(8,128)S(1)} %bitcast.610, f32[8,32,512]{2,1,0:T(8,128)S(1)} %get-tuple-element.71.text_ref, f32[9,16,128]{2,1,0:T(8,128)S(1)} %get-tuple-element.72.lower_ref), custom_call_target="tpu_custom_call" | custom-call | flops 8000000000 | bytes 1048576 | tf_op jit(solution)/shard_map/coupling/pallas_call | solution.py:699
  84.1 7.3 %all-to-all-done.1 = f32[256,2,1,128]{3,1,2,0:T(2,128)S(1)} async-done(((f32[256,2,1,128]{3,1,2,0:T(2,128)}), f32[256,2,1,128]{3,1,2,0:T(2,128)S(1)}, u32[]{:S(2)}, u32[]{:S(2)}) %all-to-all-start.1) | async-done | bytes 262176 | tf_op jit(solution)/shard_map/all_to_all | solution.py:649
  91.4 1.2 step.4
  92.7 21.5 %all_to_all.30 = f32[256,2,1,128]{3,1,2,0:T(2,128)S(1)} all-to-all(f32[256,2,1,128]{3,1,2,0:T(2,128)S(1)} %bitcast.617), channel_id=1, replica_groups=mesh['cam'=32,'pt'=8] {'cam','pt'}, dimensions={0} | all-to-all | bytes 524288 | tf_op jit(solution)/shard_map/all_to_all | solution.py:649
  114.2 1.2 step.5
  115.5 33.7 %all_to_all.31 = f32[256,2,1,128]{3,1,2,0:T(2,128)S(1)} all-to-all(f32[256,2,1,128]{3,1,2,0:T(2,128)S(1)} %bitcast.618), channel_id=1, replica_groups=mesh['cam'=32,'pt'=8] {'cam','pt'}, dimensions={0} | all-to-all | bytes 524288 | tf_op jit(solution)/shard_map/all_to_all | solution.py:649
  149.2 1.4 step.6
  150.6 21.1 %all_to_all.32 = f32[256,2,1,128]{3,1,2,0:T(2,128)S(1)} all-to-all(f32[256,2,1,128]{3,1,2,0:T(2,128)S(1)} %bitcast.616), channel_id=1, replica_groups=mesh['cam'=32,'pt'=8] {'cam','pt'}, dimensions={0} | all-to-all | bytes 524288 | tf_op jit(solution)/shard_map/all_to_all | solution.py:649
  171.7 2.0 step.7
  173.7 5.9 %all-to-all-start.5 = ((f32[256,3,1,128]{3,2,1,0:T(1,128)}), f32[256,3,1,128]{3,2,1,0:T(1,128)S(1)}, u32[]{:S(2)}, u32[]{:S(2)}) async-start(f32[256,3,1,128]{3,2,1,0:T(1,128)} %bitcast.132), calls=%async_computation.5 | async-start | bytes 786432 | tf_op jit(solution)/shard_map/all_to_all | solution.py:649
  179.6 0.5 slice.280
  180.7 16.1 %all-to-all-done.5 = f32[256,3,1,128]{3,2,1,0:T(1,128)S(1)} async-done(((f32[256,3,1,128]{3,2,1,0:T(1,128)}), f32[256,3,1,128]{3,2,1,0:T(1,128)S(1)}, u32[]{:S(2)}, u32[]{:S(2)}) %all-to-all-start.5) | async-done | bytes 393248 | tf_op jit(solution)/shard_map/all_to_all | solution.py:649
  196.8 0.0 copy-done.1
  196.8 0.0 copy-done.2
  196.8 0.0 copy-done.3
  196.8 0.0 copy-done.7
  196.8 0.0 copy-done.9
  196.8 2.2 %finish.1 = (f32[9,128]{1,0:T(8,128)}, f32[9,128]{1,0:T(8,128)S(1)}, f32[3,512]{1,0:T(4,128)S(1)}) custom-call(f32[768,128]{1,0:T(8,128)S(1)} %bitcast.611, f32[8,512]{1,0:T(8,128)S(1)} %get-tuple-element.88.place_ref, f32[7,16,128]{2,1,0:T(8,128)S(1)} %get-tuple-element.89.state_ref, f32[288,128]{1,0:T(8,128)S(1)} %bitcast.634, f32[96,128]{1,0:T(8,128)S(1)} %bitcast.642, ...), custom_call_target="tpu_custom_call" | custom-call | tf_op jit(solution)/shard_map/finish/pallas_call | solution.py:723
  199.0 0.0 copy-done.10
  199.0 0.0 copy-done.11
  199.0 0.0 copy-start.12
  199.0 0.6 copy-done.12
  199.6 0.0 copy-start.13
  199.6 0.6 copy-done.13
  (2 shorter events, 0.0 us)
Async XLA Ops:
  7.2 0.8 copy-start
  15.3 51.7 %all-to-all-start = ((f32[256,10,1,128]{3,2,1,0:T(1,128)}), f32[256,10,1,128]{3,2,1,0:T(1,128)S(1)}, u32[]{:S(2)}, u32[]{:S(2)}) async-start(f32[256,10,1,128]{3,2,1,0:T(1,128)} %bitcast.117), calls=%async_computation | async-start | bytes 2621440 | tf_op jit(solution)/shard_map/all_to_all | solution.py:649
  69.3 22.2 %all-to-all-start.1 = ((f32[256,2,1,128]{3,1,2,0:T(2,128)}), f32[256,2,1,128]{3,1,2,0:T(2,128)S(1)}, u32[]{:S(2)}, u32[]{:S(2)}) async-start(f32[256,2,1,128]{3,1,2,0:T(2,128)} %bitcast.120), calls=%async_computation.1 | async-start | bytes 524288 | tf_op jit(solution)/shard_map/all_to_all | solution.py:649
  76.3 120.5 %copy-start.1 = (f32[4,18,512]{2,0,1:T(4,128)S(1)}, f32[4,18,512]{2,0,1:T(4,128)}, u32[]{:S(2)}) copy-start(f32[4,18,512]{2,0,1:T(4,128)} %param.10) | copy-start | bytes 442372
  76.3 120.5 %copy-start.2 = (f32[4,6,512]{2,0,1:T(4,128)S(1)}, f32[4,6,512]{2,0,1:T(4,128)}, u32[]{:S(2)}) copy-start(f32[4,6,512]{2,0,1:T(4,128)} %param.11) | copy-start | bytes 147460
  76.3 120.5 %copy-start.3 = (f32[9,512]{1,0:T(8,128)S(1)}, f32[9,512]{1,0:T(8,128)}, u32[]{:S(2)}) copy-start(f32[9,512]{1,0:T(8,128)} %vi_ref.3) | copy-start | bytes 55300
  76.3 120.5 %copy-start.7 = (f32[4,2,512]{2,1,0:T(2,128)S(1)}, f32[4,2,512]{2,1,0:T(2,128)}, u32[]{:S(2)}) copy-start(f32[4,2,512]{2,1,0:T(2,128)} %rs_ref.3) | copy-start | bytes 49156
  76.3 120.5 %copy-start.9 = (s32[4,512]{1,0:T(4,128)S(1)}, s32[4,512]{1,0:T(4,128)}, u32[]{:S(2)}) copy-start(s32[4,512]{1,0:T(4,128)} %used_ref.3) | copy-start | bytes 24580
  76.3 122.7 %copy-start.10 = (s32[4,512]{1,0:T(4,128)S(1)}, s32[4,512]{1,0:T(4,128)}, u32[]{:S(2)}) copy-start(s32[4,512]{1,0:T(4,128)} %cam_ref.1) | copy-start | bytes 24580
  76.4 122.6 %copy-start.11 = (s32[12,128]{1,0:T(8,128)S(1)}, s32[12,128]{1,0:T(8,128)}, u32[]{:S(2)}) copy-start(s32[12,128]{1,0:T(8,128)} %pattern_ref.3) | copy-start | bytes 18436
  173.7 23.1 %all-to-all-start.5 = ((f32[256,3,1,128]{3,2,1,0:T(1,128)}), f32[256,3,1,128]{3,2,1,0:T(1,128)S(1)}, u32[]{:S(2)}, u32[]{:S(2)}) async-start(f32[256,3,1,128]{3,2,1,0:T(1,128)} %bitcast.132), calls=%async_computation.5 | async-start | bytes 786432 | tf_op jit(solution)/shard_map/all_to_all | solution.py:649
  199.0 0.6 copy-start.12
  199.6 0.6 copy-start.13
where the time goes:
time: 209 us; the launch traced here: 207 us
  blocking collectives  76.3 us (37%)
  waiting for transfers between devices  57.2 us (27%)
  starting transfers between devices  28.6 us (14%)
  Pallas kernels  27.6 us (13%)
  between operations  15 us (7%)
  local copies, waits for them, and re-layouts  2.52 us (1%)
    all_to_all x3, blocking collectives, exchange(): lax.all_to_all(message.reshape(devices, width, 1, 128), BOTH, split_axis=...  76.3 us
    all_to_all x3, waiting for transfers between devices, exchange(): lax.all_to_all(message.reshape(devices, width, 1, 128), BOTH, split_axis=...  57.2 us
    all_to_all x3, starting transfers between devices, exchange(): lax.all_to_all(message.reshape(devices, width, 1, 128), BOTH, split_axis=...  28.6 us
    pallas_call x1, Pallas kernels, per_device(): call(coupling_kernel, (shape(NBR, CELL, cam_dev), shape(OBS_CAP, devices,...  7.76 us
    pallas_call x1, Pallas kernels, per_device(): call(functools.partial(pack_kernel, devices, shift), (shape(devices * 10,...  7.42 us
    pallas_call x4, Pallas kernels, per_device(): call(functools.partial(step_kernel, index), (shape(7, 16, cam_dev), shape...  5.88 us
  transfers between devices with their start and end apart: 3, of which 3 were waited for; matrix products, arithmetic and copies ran while one was open for 0% of the time, Pallas kernels for 5%

commit v1 on v0

--- a/solution.py
+++ b/solution.py
@@ -454,12 +454,13 @@
     devices = got_ref.shape[0] // rows
     turned = [got_ref[pl.ds(h, devices, stride=rows), :].T for h in range(rows)]
     mark = one_hot(iota((devices, sources.shape[1]), 0).astype(F32) == sources)
-    split = jnp.concatenate([piece for plane in turned for piece in pieces(plane)], axis=0)
-    taken = dot_nn(split, mark)
-    taken = [
-        taken[at : at + 128] + taken[at + 128 : at + 256] + taken[at + 256 : at + 384]
-        for at in range(0, 384 * rows, 384)
-    ]
+    parts = turned[:2] + [jnp.concatenate([plane[0:32], plane[64:80]], axis=0) for plane in turned[2:]]
+    split = jnp.concatenate([piece for part in parts for piece in pieces(part)], axis=0)
+    sums = dot_nn(split, mark)
+    taken, at = [], 0
+    for part in parts:
+        taken.append(folded(sums[at : at + 3 * part.shape[0]]))
+        at += 3 * part.shape[0]
     sums = [jnp.sum(plane[126 + i : 127 + i], axis=1, keepdims=True) for plane in turned for i in range(2)]
     return taken, sums
 
@@ -540,7 +541,17 @@
     step_ref[...] = (state_ref[0] + alpha * state_ref[3])[:9]
     rest_ref[...] = (state_ref[1] - alpha * state_ref[4])[:9]
     part = quotient(within, PAIRS)
-    taken = jnp.where(part == 0, taken[0], jnp.where(part == 1, taken[1], taken[2]))
+    first = jnp.where(part == 0, taken[0], taken[1])
+    third = part == 2
+    taken = jnp.concatenate(
+        [
+            jnp.where(third, taken[2][:32], first[:32]),
+            first[32:64],
+            jnp.where(third, taken[2][32:], first[64:80]),
+            first[80:],
+        ],
+        axis=0,
+    )
     groups = 2.0 * (within - part * PAIRS)
     moved = pick(taken, groups) + alpha * pick(taken, groups + 1.0)
     reduced = [jnp.zeros((1, npts), F32) for _ in range(3)]

time: 209 us -> 208 us (level)
  no operation moved by 1% of the time
where the time goes in v1:
time: 208 us; the launch traced here: 207 us
  blocking collectives  76.2 us (37%)
  waiting for transfers between devices  57.2 us (28%)
  starting transfers between devices  28.6 us (14%)
  Pallas kernels  27 us (13%)
  between operations  15 us (7%)
  local copies, waits for them, and re-layouts  2.51 us (1%)
    all_to_all x3, blocking collectives, exchange(): lax.all_to_all(message.reshape(devices, width, 1, 128), BOTH, split_axis=...  76.2 us
    all_to_all x3, waiting for transfers between devices, exchange(): lax.all_to_all(message.reshape(devices, width, 1, 128), BOTH, split_axis=...  57.2 us
    all_to_all x3, starting transfers between devices, exchange(): lax.all_to_all(message.reshape(devices, width, 1, 128), BOTH, split_axis=...  28.6 us
    pallas_call x1, Pallas kernels, per_device(): call(coupling_kernel, (shape(NBR, CELL, cam_dev), shape(OBS_CAP, devices,...  7.76 us
    pallas_call x1, Pallas kernels, per_device(): call(functools.partial(pack_kernel, devices, shift), (shape(devices * 10,...  7.42 us
    pallas_call x4, Pallas kernels, per_device(): call(functools.partial(step_kernel, index), (shape(7, 16, cam_dev), shape...  5.87 us
  transfers between devices with their start and end apart: 3, of which 3 were waited for; matrix products, arithmetic and copies ran while one was open for 0% of the time, Pallas kernels for 5%

profile of v1, /device:TPU:1, one launch (start us, length us, event | category | flops | bytes accessed | tf_op | source)
XLA Modules:
  0.0 206.6 jit_solution(2315476964949359390)
XLA Ops:
  7.2 0.0 copy-start
  7.2 0.7 copy-done
  7.9 7.4 %pack.1 = (f32[2560,128]{1,0:T(8,128)}, f32[8,512]{1,0:T(8,128)S(1)}, f32[256,128]{1,0:T(8,128)S(1)}) custom-call(f32[288,128]{1,0:T(8,128)} %bitcast.633, f32[96,128]{1,0:T(8,128)} %bitcast.641, f32[4,2,512]{2,1,0:T(2,128)} %rs_ref.3, f32[9,512]{1,0:T(8,128)} %vi_ref.3, s32[4,512]{1,0:T(4,128)} %cam_ref.1, s32[4,4,512]{2,1,0:T(4,128)S(1)} %copy-done, ...), custom_call_target="tpu_custom_call" | custom-call | tf_op jit(solution)/shard_map/pack/pallas_call | solution.py:678
  15.3 15.7 %all-to-all-start = ((f32[256,10,1,128]{3,2,1,0:T(1,128)}), f32[256,10,1,128]{3,2,1,0:T(1,128)S(1)}, u32[]{:S(2)}, u32[]{:S(2)}) async-start(f32[256,10,1,128]{3,2,1,0:T(1,128)} %bitcast.117), calls=%async_computation | async-start | bytes 2621440 | tf_op jit(solution)/shard_map/all_to_all | solution.py:660
  31.0 2.1 %place.1 = (f32[1,1536]{1,0:T(1,128)S(1)}, f32[1,1536]{1,0:T(1,128)S(1)}, f32[1,1536]{1,0:T(1,128)S(1)}, s32[32,256]{1,0:T(8,128)S(1)}, f32[2,256]{1,0:T(2,128)S(1)}) custom-call(s32[12,128]{1,0:T(8,128)} %pattern_ref.3, f32[256,128]{1,0:T(8,128)S(1)} %get-tuple-element.64.rank_ref), custom_call_target="tpu_custom_call" | custom-call | flops 4000000000 | bytes 1048576 | tf_op jit(solution)/shard_map/place/pallas_call | solution.py:687
  33.1 33.9 %all-to-all-done = f32[256,10,1,128]{3,2,1,0:T(1,128)S(1)} async-done(((f32[256,10,1,128]{3,2,1,0:T(1,128)}), f32[256,10,1,128]{3,2,1,0:T(1,128)S(1)}, u32[]{:S(2)}, u32[]{:S(2)}) %all-to-all-start) | async-done | bytes 1310752 | tf_op jit(solution)/shard_map/all_to_all | solution.py:660
  67.0 2.3 %diagonal.1 = (f32[8,32,512]{2,1,0:T(8,128)S(1)}, f32[96,128]{1,0:T(8,128)S(1)}, f32[9,16,128]{2,1,0:T(8,128)S(1)}, f32[7,16,128]{2,1,0:T(8,128)S(1)}, f32[512,128]{1,0:T(8,128)}) custom-call(f32[2560,128]{1,0:T(8,128)S(1)} %bitcast.609, s32[32,256]{1,0:T(8,128)S(1)} %get-tuple-element.65.choice_ref, f32[2,256]{1,0:T(2,128)S(1)} %get-tuple-element.66.count_ref), custom_call_target="tpu_custom_call" | custom-call | tf_op jit(solution)/shard_map/diagonal/pallas_call | solution.py:699
  69.3 7.0 %all-to-all-start.1 = ((f32[256,2,1,128]{3,1,2,0:T(2,128)}), f32[256,2,1,128]{3,1,2,0:T(2,128)S(1)}, u32[]{:S(2)}, u32[]{:S(2)}) async-start(f32[256,2,1,128]{3,1,2,0:T(2,128)} %bitcast.120), calls=%async_computation.1 | async-start | bytes 524288 | tf_op jit(solution)/shard_map/all_to_all | solution.py:660
  76.3 0.0 copy-start.1
  76.3 0.0 copy-start.2
  76.3 0.0 copy-start.3
  76.3 0.0 copy-start.7
  76.3 0.0 copy-start.9
  76.3 0.0 copy-start.10
  76.4 0.0 copy-start.11
  76.4 7.8 %coupling.1 = (f32[12,96,128]{2,1,0:T(8,128)S(1)}, s32[16,256]{1,0:T(8,128)S(1)}, f32[96,128]{1,0:T(8,128)S(1)}) custom-call(f32[2560,128]{1,0:T(8,128)S(1)} %bitcast.610, f32[8,32,512]{2,1,0:T(8,128)S(1)} %get-tuple-element.71.text_ref, f32[9,16,128]{2,1,0:T(8,128)S(1)} %get-tuple-element.72.lower_ref), custom_call_target="tpu_custom_call" | custom-call | flops 8000000000 | bytes 1048576 | tf_op jit(solution)/shard_map/coupling/pallas_call | solution.py:710
  84.1 7.3 %all-to-all-done.1 = f32[256,2,1,128]{3,1,2,0:T(2,128)S(1)} async-done(((f32[256,2,1,128]{3,1,2,0:T(2,128)}), f32[256,2,1,128]{3,1,2,0:T(2,128)S(1)}, u32[]{:S(2)}, u32[]{:S(2)}) %all-to-all-start.1) | async-done | bytes 262176 | tf_op jit(solution)/shard_map/all_to_all | solution.py:660
  91.4 1.2 step.4
  92.7 21.5 %all_to_all.30 = f32[256,2,1,128]{3,1,2,0:T(2,128)S(1)} all-to-all(f32[256,2,1,128]{3,1,2,0:T(2,128)S(1)} %bitcast.617), channel_id=1, replica_groups=mesh['cam'=32,'pt'=8] {'cam','pt'}, dimensions={0} | all-to-all | bytes 524288 | tf_op jit(solution)/shard_map/all_to_all | solution.py:660
  114.2 1.2 step.5
  115.5 33.6 %all_to_all.31 = f32[256,2,1,128]{3,1,2,0:T(2,128)S(1)} all-to-all(f32[256,2,1,128]{3,1,2,0:T(2,128)S(1)} %bitcast.618), channel_id=1, replica_groups=mesh['cam'=32,'pt'=8] {'cam','pt'}, dimensions={0} | all-to-all | bytes 524288 | tf_op jit(solution)/shard_map/all_to_all | solution.py:660
  149.1 1.4 step.6
  150.5 21.1 %all_to_all.32 = f32[256,2,1,128]{3,1,2,0:T(2,128)S(1)} all-to-all(f32[256,2,1,128]{3,1,2,0:T(2,128)S(1)} %bitcast.616), channel_id=1, replica_groups=mesh['cam'=32,'pt'=8] {'cam','pt'}, dimensions={0} | all-to-all | bytes 524288 | tf_op jit(solution)/shard_map/all_to_all | solution.py:660
  171.6 2.0 step.7
  173.6 5.9 %all-to-all-start.5 = ((f32[256,3,1,128]{3,2,1,0:T(1,128)}), f32[256,3,1,128]{3,2,1,0:T(1,128)S(1)}, u32[]{:S(2)}, u32[]{:S(2)}) async-start(f32[256,3,1,128]{3,2,1,0:T(1,128)} %bitcast.132), calls=%async_computation.5 | async-start | bytes 786432 | tf_op jit(solution)/shard_map/all_to_all | solution.py:660
  179.5 0.5 slice.280
  180.6 16.1 %all-to-all-done.5 = f32[256,3,1,128]{3,2,1,0:T(1,128)S(1)} async-done(((f32[256,3,1,128]{3,2,1,0:T(1,128)}), f32[256,3,1,128]{3,2,1,0:T(1,128)S(1)}, u32[]{:S(2)}, u32[]{:S(2)}) %all-to-all-start.5) | async-done | bytes 393248 | tf_op jit(solution)/shard_map/all_to_all | solution.py:660
  196.7 0.0 copy-done.1
  196.7 0.0 copy-done.2
  196.7 0.0 copy-done.3
  196.7 0.0 copy-done.7
  196.7 0.0 copy-done.9
  196.7 1.6 finish.1
  198.3 0.0 copy-done.10
  198.3 0.0 copy-done.11
  198.3 0.0 copy-start.12
  198.4 0.6 copy-done.12
  199.0 0.0 copy-start.13
  199.0 0.6 copy-done.13
  (2 shorter events, 0.0 us)
Async XLA Ops:
  7.2 0.8 copy-start
  15.3 51.7 %all-to-all-start = ((f32[256,10,1,128]{3,2,1,0:T(1,128)}), f32[256,10,1,128]{3,2,1,0:T(1,128)S(1)}, u32[]{:S(2)}, u32[]{:S(2)}) async-start(f32[256,10,1,128]{3,2,1,0:T(1,128)} %bitcast.117), calls=%async_computation | async-start | bytes 2621440 | tf_op jit(solution)/shard_map/all_to_all | solution.py:660
  69.3 22.2 %all-to-all-start.1 = ((f32[256,2,1,128]{3,1,2,0:T(2,128)}), f32[256,2,1,128]{3,1,2,0:T(2,128)S(1)}, u32[]{:S(2)}, u32[]{:S(2)}) async-start(f32[256,2,1,128]{3,1,2,0:T(2,128)} %bitcast.120), calls=%async_computation.1 | async-start | bytes 524288 | tf_op jit(solution)/shard_map/all_to_all | solution.py:660
  76.3 120.4 %copy-start.1 = (f32[4,18,512]{2,0,1:T(4,128)S(1)}, f32[4,18,512]{2,0,1:T(4,128)}, u32[]{:S(2)}) copy-start(f32[4,18,512]{2,0,1:T(4,128)} %param.10) | copy-start | bytes 442372
  76.3 120.4 %copy-start.2 = (f32[4,6,512]{2,0,1:T(4,128)S(1)}, f32[4,6,512]{2,0,1:T(4,128)}, u32[]{:S(2)}) copy-start(f32[4,6,512]{2,0,1:T(4,128)} %param.11) | copy-start | bytes 147460
  76.3 120.4 %copy-start.3 = (f32[9,512]{1,0:T(8,128)S(1)}, f32[9,512]{1,0:T(8,128)}, u32[]{:S(2)}) copy-start(f32[9,512]{1,0:T(8,128)} %vi_ref.3) | copy-start | bytes 55300
  76.3 120.4 %copy-start.7 = (f32[4,2,512]{2,1,0:T(2,128)S(1)}, f32[4,2,512]{2,1,0:T(2,128)}, u32[]{:S(2)}) copy-start(f32[4,2,512]{2,1,0:T(2,128)} %rs_ref.3) | copy-start | bytes 49156
  76.3 120.4 %copy-start.9 = (s32[4,512]{1,0:T(4,128)S(1)}, s32[4,512]{1,0:T(4,128)}, u32[]{:S(2)}) copy-start(s32[4,512]{1,0:T(4,128)} %used_ref.3) | copy-start | bytes 24580
  76.3 122.0 %copy-start.10 = (s32[4,512]{1,0:T(4,128)S(1)}, s32[4,512]{1,0:T(4,128)}, u32[]{:S(2)}) copy-start(s32[4,512]{1,0:T(4,128)} %cam_ref.1) | copy-start | bytes 24580
  76.4 122.0 %copy-start.11 = (s32[12,128]{1,0:T(8,128)S(1)}, s32[12,128]{1,0:T(8,128)}, u32[]{:S(2)}) copy-start(s32[12,128]{1,0:T(8,128)} %pattern_ref.3) | copy-start | bytes 18436
  173.6 23.1 %all-to-all-start.5 = ((f32[256,3,1,128]{3,2,1,0:T(1,128)}), f32[256,3,1,128]{3,2,1,0:T(1,128)S(1)}, u32[]{:S(2)}, u32[]{:S(2)}) async-start(f32[256,3,1,128]{3,2,1,0:T(1,128)} %bitcast.132), calls=%async_computation.5 | async-start | bytes 786432 | tf_op jit(solution)/shard_map/all_to_all | solution.py:660
  198.3 0.6 copy-start.12
  199.0 0.6 copy-start.13
